TPU v7x, 32 devices: a whole 2x2x4 slice. The times are simulated.
32 devices in a mesh: region: 8 (over z, y), sub: 4 (over x, core).
Axes of the slice: x: 2, y: 2, z: 4, core: 2. Of those that a mesh axis runs over, the one named last changes fastest.
Arguments:
- mode_rows: bfloat16 [16384, 4096], P(('region', 'sub')), may hold values from -0.09375 to 0.09375
- input_rows: bfloat16 [512, 4096], P(('region', 'sub')), may hold values from -0.25 to 0.25
- input_factor: bfloat16 [512, 128], P(('region', 'sub')), may hold values from -6 to 6
- mode_freq: float32 [4096], replicated, may hold values from 0.5 to 2
- mode_damping: float32 [4096], replicated, may hold values from 0.02 to 0.2
- line_freq: float32 [2], replicated, may hold values from 0.6 to 1.6
- boundary_rows: int32 [4096], P(('region', 'sub')), may hold values from 0 to 511
- connectivity: int32 [4, 16384], P(None, ('region', 'sub')), may hold values from 0 to 639
- stress_coef: float32 [4, 16384], P(None, ('region', 'sub')), may hold values from -3 to 3
Outputs:
- stress_psd: float32 [2, 16384], P(None, ('region', 'sub'))
Inputs may be any that keep to these rules, and one draw needn't show every extreme that they name: `boundary_rows`: local row numbers of the sending device. `connectivity`: rows of the node table of the element's device.
All inputs are finite; a program needn't handle non-finite values.
Results may differ from a plain program's by a relative error of at most 0.0013.
Values may be sent and summed in bfloat16 or wider, within the bound.
No kernel may reach another device: no remote copies, remote signals or barrier semaphores. Data moves between devices by JAX's collectives and lax.ppermute only.
A program may use at most 64 MiB of HBM per device.

v0:
```python
import jax
import jax.numpy as jnp
from jax import lax
from jax.sharding import PartitionSpec as P


def extended(cells, sides, width):
    for axis, dim in sides:
        count = lax.axis_size(axis)
        ends = count - 1
        head = lax.slice_in_dim(cells, 0, width, axis=dim)
        tail = lax.slice_in_dim(cells, cells.shape[dim] - width, cells.shape[dim], axis=dim)
        cells = jnp.concatenate(
            [
                lax.ppermute(tail, axis, [(i, (i + 1) % count) for i in range(ends)]),
                cells,
                lax.ppermute(head, axis, [((i + 1) % count, i) for i in range(ends)]),
            ],
            axis=dim,
        )
    return cells


def modal_gain(mode_freq, mode_damping, line_omega):
    detune = mode_freq * mode_freq - line_omega * line_omega
    damped = 2.0 * mode_damping * mode_freq * line_omega
    magnitude = detune * detune + damped * damped
    return (detune / magnitude, -damped / magnitude)


def apply_gain(summed, gain_real, gain_imag):
    half_cols = summed.shape[1] // 2
    forced_real = summed[:, :half_cols]
    forced_imag = summed[:, half_cols:]
    out_real = gain_real[:, None] * forced_real - gain_imag[:, None] * forced_imag
    out_imag = gain_real[:, None] * forced_imag + gain_imag[:, None] * forced_real
    return jnp.concatenate([out_real, out_imag], axis=1).astype(jnp.bfloat16)


def scale_lines(summed, mode_freq, mode_damping, line_freq, columns):
    pieces = []
    for line_no in range(line_freq.shape[0]):
        gain_real, gain_imag = modal_gain(mode_freq, mode_damping, line_freq[line_no])
        pieces.append(
            apply_gain(summed[:, line_no * columns : (line_no + 1) * columns], gain_real, gain_imag)
        )
    return jnp.concatenate(pieces, axis=1)


def local(
    mode_rows,
    input_rows,
    input_factor,
    mode_freq,
    mode_damping,
    line_freq,
    boundary_rows,
    connectivity,
    stress_coef,
):
    mode_count = input_rows.shape[1]
    line_count = line_freq.shape[0]
    width_all = input_factor.shape[1]
    columns = width_all // line_count
    partial_value = lax.dot_general(
        input_rows, input_factor, (((0,), (0,)), ((), ())), preferred_element_type=jnp.float32
    )
    summed = lax.psum(
        partial_value.reshape(mode_count // 2, 2 * width_all), ("region", "sub")
    ).reshape(mode_count, width_all)
    pseudo = scale_lines(summed, mode_freq, mode_damping, line_freq, columns)
    responses = jnp.dot(mode_rows, pseudo, preferred_element_type=jnp.float32).astype(jnp.bfloat16)
    rim_rows = boundary_rows.shape[0] // 2
    export = responses[boundary_rows]
    padded = extended(export, ((("region", "sub"), 0),), rim_rows)
    node_table = jnp.concatenate([padded[:rim_rows], responses, padded[3 * rim_rows :]], axis=0)
    stress = stress_coef[0][:, None] * node_table[connectivity[0]].astype(jnp.float32)
    for corner in range(1, connectivity.shape[0]):
        stress = stress + stress_coef[corner][:, None] * node_table[connectivity[corner]].astype(
            jnp.float32
        )
    squares = stress * stress
    power = jnp.stack(
        [
            jnp.mean(squares[:, line_no * columns : (line_no + 1) * columns], axis=1)
            for line_no in range(line_count)
        ],
        axis=0,
    )
    return power


def solution(mesh):
    placed = (
        P(("region", "sub"), None),
        P(("region", "sub"), None),
        P(("region", "sub"), None),
        P(),
        P(),
        P(),
        P(("region", "sub")),
        P(None, ("region", "sub")),
        P(None, ("region", "sub")),
    )
    return jax.shard_map(
        local, mesh=mesh, in_specs=placed, out_specs=P(None, ("region", "sub")), check_vma=False
    )
```

profile of v0, /device:TPU:8, one launch (start us, length us, event | category | flops | bytes accessed | tf_op | source)
XLA Modules:
  0.0 176.9 jit_solution(9402711285460344023)
XLA Ops:
  6.5 0.0 copy-start
  6.5 0.0 copy-start.5
  6.5 0.0 copy-start.6
  6.5 0.0 copy-start.3
  6.5 0.0 copy-start.4
  6.5 0.0 copy-start.1
  6.6 0.0 copy-start.2
  6.6 0.0 all-reduce.2.cloned.1.call-start
  6.6 0.8 copy-done
  7.4 2.5 %fusion.14 = f32[4096,128]{0,1:T(8,128)} fusion(bf16[16,4096]{1,0:T(8,128)(2,1)S(1)} %copy-done, bf16[16,128]{1,0:T(8,128)(2,1)} %param.11), kind=kOutput, calls=%fused_computation.46 | convolution fusion | flops 16777216 | bytes 2232320 | tf_op jit(solution)/shard_map/dot_general | solution.py:65
  9.9 0.0 all-reduce.2.cloned.1.call-update
  9.9 0.0 copy-done.5
  10.0 0.6 fusion.13
  10.5 0.0 copy-done.6
  13.0 0.0 copy-done.3
  13.1 0.0 copy-done.4
  13.1 0.0 copy-done.1
  13.1 0.0 copy-done.2
  13.1 1.2 fusion.9
  14.4 133.2 %all-reduce.2.cloned.1.call-done = f32[4096,128]{0,1:T(8,128)} async-done(((f32[4096,128]{0,1:T(8,128)}), f32[4096,128]{0,1:T(8,128)}) %all-reduce.2.cloned.1.call-update) | async-done | bytes 2097168 | tf_op jit(solution)/shard_map/psum | solution.py:68
  147.6 1.8 %subtract_convert_fusion.1 = (bf16[4096,32]{0,1:T(8,128)(2,1)S(1)}, bf16[4096,32]{0,1:T(8,128)(2,1)S(1)}, bf16[4096,32]{0,1:T(8,128)(2,1)S(1)}, bf16[4096,32]{0,1:T(8,128)(2,1)S(1)}) fusion(f32[4096,128]{0,1:T(8,128)} %all-reduce.2.cloned.1.call-done, f32[4096]{0:T(1024)S(1)} %get-tuple-element.18, f32[4096]{0:T(1024)S(1)} %get-tuple-element.15, ...), kind=kLoop, calls=%fused_computation.17 | loop fusion | flops 2097152 | bytes 3211264 | tf_op jit(solution)/shard_map/convert.2
  149.4 3.7 %fusion = bf16[512,128]{0,1:T(8,128)(2,1)S(1)} fusion(bf16[512,4096]{1,0:T(8,128)(2,1)} %param.9, bf16[4096,32]{0,1:T(8,128)(2,1)S(1)} %get-tuple-element.11, bf16[4096,32]{0,1:T(8,128)(2,1)S(1)} %get-tuple-element.12, bf16[4096,32]{0,1:T(8,128)(2,1)S(1)} %get-tuple-element.8, bf16[4096,32]{0,1:T(8,128)(2,1)S(1)} %get-tuple-element.7), kind=kOutput, calls=%fused_computation.6 | convolution fusion | flops 541130752 | bytes 5373952 | tf_op jit(solution)/shard_map/dot_general | solution.py:72
  153.1 0.1 copy.25
  153.2 0.7 gather_fusion
  153.9 0.1 copy.34
  154.1 1.9 %collective-permute-start.1 = (bf16[64,128]{0,1:T(8,128)(2,1)S(1)}, bf16[64,128]{0,1:T(8,128)(2,1)S(1)}, u32[]{:S(2)}, u32[]{:S(2)}) collective-permute-start(bf16[64,128]{0,1:T(8,128)(2,1)S(1)} %copy.34), channel_id=1, source_target_pairs={{1,0},{2,1},{3,2},{4,3},{5,4},{6,5},{7,6},{8,7},{9,8},{10,9},{11,1... | collective-permute-start | bytes 49160 | tf_op jit(solution)/shard_map/ppermute | solution.py:17
  156.0 0.1 copy.33
  156.1 2.4 %collective-permute-start = (bf16[64,128]{0,1:T(8,128)(2,1)S(1)}, bf16[64,128]{0,1:T(8,128)(2,1)S(1)}, u32[]{:S(2)}, u32[]{:S(2)}) collective-permute-start(bf16[64,128]{0,1:T(8,128)(2,1)S(1)} %copy.33), channel_id=1, source_target_pairs={{0,1},{1,2},{2,3},{3,4},{4,5},{5,6},{6,7},{7,8},{8,9},{9,10},{10,1... | collective-permute-start | bytes 49160 | tf_op jit(solution)/shard_map/ppermute | solution.py:15
  158.5 0.0 collective-permute-done.1
  158.5 4.6 %collective-permute-done = bf16[64,128]{0,1:T(8,128)(2,1)S(1)} collective-permute-done((bf16[64,128]{0,1:T(8,128)(2,1)S(1)}, bf16[64,128]{0,1:T(8,128)(2,1)S(1)}, u32[]{:S(2)}, u32[]{:S(2)}) %collective-permute-start) | collective-permute-done | bytes 16416 | tf_op jit(solution)/shard_map/ppermute | solution.py:15
  163.1 0.1 pad_maximum_fusion
  163.3 0.2 copy.28
  163.4 1.3 gather_fusion.4
  164.8 1.3 gather_fusion.3
  166.1 1.3 gather_fusion.2
  167.5 1.3 gather_fusion.1
  168.8 0.3 add_multiply_fusion
  169.2 0.3 slice_reduce_fusion.1
  169.5 0.6 pad_maximum_fusion.1
  (10 shorter events, 0.1 us)
Async XLA Ops:
  6.5 0.9 copy-start
  6.5 3.4 %copy-start.5 = (f32[2]{0:T(128)S(1)}, f32[2]{0:T(128)}, u32[]{:S(2)}) copy-start(f32[2]{0:T(128)} %param.14) | copy-start | bytes 28
  6.5 4.0 %copy-start.6 = (s32[128]{0:T(128)S(1)}, s32[128]{0:T(128)}, u32[]{:S(2)}) copy-start(s32[128]{0:T(128)} %param.15) | copy-start | bytes 1540
  6.5 6.5 %copy-start.3 = (s32[4,512]{1,0:T(4,128)S(1)}, s32[4,512]{1,0:T(4,128)}, u32[]{:S(2)}) copy-start(s32[4,512]{1,0:T(4,128)} %param.16) | copy-start | bytes 24580
  6.5 6.5 %copy-start.4 = (f32[4,512]{1,0:T(4,128)S(1)}, f32[4,512]{1,0:T(4,128)}, u32[]{:S(2)}) copy-start(f32[4,512]{1,0:T(4,128)} %param.17) | copy-start | bytes 24580
  6.5 6.6 %copy-start.1 = (f32[4096]{0:T(1024)S(1)}, f32[4096]{0:T(1024)}, u32[]{:S(2)}) copy-start(f32[4096]{0:T(1024)} %param.12) | copy-start | bytes 49156
  6.6 6.6 %copy-start.2 = (f32[4096]{0:T(1024)S(1)}, f32[4096]{0:T(1024)}, u32[]{:S(2)}) copy-start(f32[4096]{0:T(1024)} %param.13) | copy-start | bytes 49156
  6.6 141.0 %all-reduce.2.cloned.1.call-start = ((), (), s32[]{:S(2)}) async-start(), calls=%async_computation | async-start | bytes 4194304 | tf_op jit(solution)/shard_map/psum | solution.py:68
  154.1 4.5 %collective-permute-start.1 = (bf16[64,128]{0,1:T(8,128)(2,1)S(1)}, bf16[64,128]{0,1:T(8,128)(2,1)S(1)}, u32[]{:S(2)}, u32[]{:S(2)}) collective-permute-start(bf16[64,128]{0,1:T(8,128)(2,1)S(1)} %copy.34), channel_id=1, source_target_pairs={{1,0},{2,1},{3,2},{4,3},{5,4},{6,5},{7,6},{8,7},{9,8},{10,9},{11,1... | collective-permute-start | bytes 49160 | tf_op jit(solution)/shard_map/ppermute | solution.py:17
  156.1 7.0 %collective-permute-start = (bf16[64,128]{0,1:T(8,128)(2,1)S(1)}, bf16[64,128]{0,1:T(8,128)(2,1)S(1)}, u32[]{:S(2)}, u32[]{:S(2)}) collective-permute-start(bf16[64,128]{0,1:T(8,128)(2,1)S(1)} %copy.33), channel_id=1, source_target_pairs={{0,1},{1,2},{2,3},{3,4},{4,5},{5,6},{6,7},{7,8},{8,9},{9,10},{10,1... | collective-permute-start | bytes 49160 | tf_op jit(solution)/shard_map/ppermute | solution.py:15
Sparse Core Ops, SparseCore 0:
  12.7 134.7 all-reduce.1
where the time goes:
time: 177 us
  waiting for transfers between devices  138 us (78%)
  between operations  16.1 us (9%)
  local copies, waits for them, and re-layouts  8.04 us (5%)
  matrix products  6.2 us (4%)
  other arithmetic  4.43 us (3%)
  starting transfers between devices  4.36 us (2%)
    psum x1, waiting for transfers between devices, local(): lax.psum(partial_value.reshape(mode_count // 2, 2 * width_all), ('region'...  133 us
    ppermute x1, waiting for transfers between devices, extended(): lax.ppermute(tail, axis, [(i, (i + 1) % count) for i in range(ends)])  4.59 us
    gather x3, local copies, waits for them, and re-layouts, local(): node_table[connectivity[corner]].astype(jnp.float32)  4.02 us
    dot_general x1, matrix products, local(): jnp.dot(mode_rows, pseudo, preferred_element_type=jnp.float32)  3.72 us
  transfers between devices with their start and end apart: 3, of which 2 were waited for; matrix products, arithmetic and copies ran while one was open for 1% of the time, Pallas kernels for 0%

commit v1 on v0

v1 whole, which is shorter than its diff:
```python
import functools

import jax
import jax.numpy as jnp
from jax import lax
from jax.experimental import pallas as pl
from jax.experimental.pallas import tpu as pltpu
from jax.sharding import PartitionSpec as P

AXES = ("region", "sub")
LANES = 128
F32 = jnp.float32
BF16 = jnp.bfloat16
VMEM_BYTES = 24 * 1024 * 1024


def whole(*_):
    return pl.BlockSpec(memory_space=pltpu.VMEM)


def modal_gain(freq, damping, omega):
    detune = freq * freq - omega * omega
    damped = 2.0 * damping * freq * omega
    magnitude = detune * detune + damped * damped
    return detune / magnitude, -damped / magnitude


def setup_kernel(boundary_ref, connect_ref, coef_ref, modes_ref, export_ref, high_ref, low_ref):
    rows = modes_ref.shape[0]
    exports = boundary_ref.shape[0]
    pick = lax.broadcasted_iota(jnp.int32, (exports, rows), 1) == boundary_ref[...]
    pick = pick.astype(F32).astype(BF16)
    step = 1024
    for start in range(0, modes_ref.shape[1], step):
        block = modes_ref[:, start : start + step]
        export_ref[:, start : start + step] = jnp.dot(
            pick, block, preferred_element_type=F32
        ).astype(BF16)
    nodes, elems = high_ref.shape
    tall = 64
    for start in range(0, nodes, tall):
        node = lax.broadcasted_iota(jnp.int32, (tall, elems), 0) + start
        total = jnp.zeros((tall, elems), F32)
        for corner in range(connect_ref.shape[0]):
            hit = node == connect_ref[corner : corner + 1, :]
            total = total + jnp.where(hit, coef_ref[corner : corner + 1, :], 0.0)
        high = total.astype(BF16)
        high_ref[start : start + tall, :] = high
        low_ref[start : start + tall, :] = (total - high.astype(F32)).astype(BF16)


def scale_transposed(forced, freq, damping, line_ref, columns):
    half = columns // 2
    pieces = []
    for line in range(line_ref.shape[0]):
        gain_real, gain_imag = modal_gain(freq, damping, line_ref[line])
        real = forced[line * columns : line * columns + half]
        imag = forced[line * columns + half : (line + 1) * columns]
        pieces.append(gain_real * real - gain_imag * imag)
        pieces.append(gain_real * imag + gain_imag * real)
    return jnp.concatenate(pieces, axis=0)


def pseudo_kernel(line_ref, freq_ref, damping_ref, got_ref, pseudo_ref, *, rows):
    devices, _, width = got_ref.shape
    me = lax.axis_index(AXES)
    shapes = got_ref[:, :rows, :].reshape(devices * rows, width)
    factor = got_ref[:, rows:, :].reshape(devices * rows, width)
    forced = lax.dot_general(
        factor, shapes, (((0,), (0,)), ((), ())), preferred_element_type=F32
    )
    columns = width // line_ref.shape[0]
    scaled = scale_transposed(
        forced, freq_ref[pl.ds(me, 1), :], damping_ref[pl.ds(me, 1), :], line_ref, columns
    )
    pseudo_ref[...] = scaled.T.astype(BF16)


def stress_kernel(own_ref, lower_ref, upper_ref, pseudo_ref, high_ref, low_ref, power_ref, total, *, lines):
    step = pl.program_id(0)

    @pl.when(step == 0)
    def _():
        total[...] = jnp.zeros_like(total)

    rim = lower_ref.shape[0]
    rows = own_ref.shape[0]
    block = pseudo_ref[...]
    total[:rim] += jnp.dot(lower_ref[...], block, preferred_element_type=F32)
    total[rim : rim + rows] += jnp.dot(own_ref[...], block, preferred_element_type=F32)
    total[rim + rows :] += jnp.dot(upper_ref[...], block, preferred_element_type=F32)

    @pl.when(step == pl.num_programs(0) - 1)
    def _():
        table = total[...].T.astype(BF16)
        stress = jnp.dot(table, high_ref[...], preferred_element_type=F32)
        stress = stress + jnp.dot(table, low_ref[...], preferred_element_type=F32)
        squares = stress * stress
        columns = squares.shape[0] // lines
        for line in range(lines):
            power_ref[line : line + 1, :] = (
                jnp.sum(squares[line * columns : (line + 1) * columns], axis=0, keepdims=True)
                / columns
            )


def setup(boundary_rows, connectivity, stress_coef, mode_rows):
    exports = boundary_rows.shape[0]
    rows, modes = mode_rows.shape
    elems = connectivity.shape[1]
    nodes = rows + exports
    return pl.pallas_call(
        setup_kernel,
        out_shape=[
            jax.ShapeDtypeStruct((exports, modes), BF16),
            jax.ShapeDtypeStruct((nodes, elems), BF16),
            jax.ShapeDtypeStruct((nodes, elems), BF16),
        ],
        in_specs=[whole()] * 4,
        out_specs=[whole()] * 3,
        compiler_params=pltpu.CompilerParams(vmem_limit_bytes=VMEM_BYTES),
        cost_estimate=pl.CostEstimate(
            flops=2 * exports * rows * modes + 8 * nodes * elems,
            bytes_accessed=2 * (rows + exports) * modes + 4 * nodes * elems,
            transcendentals=0,
        ),
        name="setup",
    )(boundary_rows.reshape(exports, 1), connectivity, stress_coef, mode_rows)


def pseudo_part(got, line_freq, mode_freq, mode_damping, rows):
    devices, _, width = got.shape
    modes = mode_freq.shape[0] // devices
    return pl.pallas_call(
        functools.partial(pseudo_kernel, rows=rows),
        out_shape=jax.ShapeDtypeStruct((modes, width), BF16),
        in_specs=[pl.BlockSpec(memory_space=pltpu.SMEM), whole(), whole(), whole()],
        out_specs=whole(),
        compiler_params=pltpu.CompilerParams(vmem_limit_bytes=VMEM_BYTES),
        cost_estimate=pl.CostEstimate(
            flops=2 * devices * rows * modes * width,
            bytes_accessed=2 * got.size,
            transcendentals=0,
        ),
        name="pseudo",
    )(line_freq, mode_freq.reshape(devices, modes), mode_damping.reshape(devices, modes), got)


def stress_part(mode_rows, lower, upper, pseudo, high, low, lines):
    rows, modes = mode_rows.shape
    rim = lower.shape[0]
    nodes, elems = high.shape
    width = pseudo.shape[1]
    step = 1024
    return pl.pallas_call(
        functools.partial(stress_kernel, lines=lines),
        out_shape=jax.ShapeDtypeStruct((lines, elems), F32),
        grid=(modes // step,),
        in_specs=[
            pl.BlockSpec((rows, step), lambda i: (0, i)),
            pl.BlockSpec((rim, step), lambda i: (0, i)),
            pl.BlockSpec((rim, step), lambda i: (0, i)),
            pl.BlockSpec((step, width), lambda i: (i, 0)),
            whole(),
            whole(),
        ],
        out_specs=whole(),
        scratch_shapes=[pltpu.VMEM((nodes, width), F32)],
        compiler_params=pltpu.CompilerParams(vmem_limit_bytes=VMEM_BYTES),
        cost_estimate=pl.CostEstimate(
            flops=2 * nodes * modes * width + 4 * nodes * elems * width,
            bytes_accessed=2 * (nodes + width) * modes + 4 * nodes * elems,
            transcendentals=0,
        ),
        name="stress",
    )(mode_rows, lower, upper, pseudo, high, low)


def pseudo_by_sum(input_rows, input_factor, mode_freq, mode_damping, line_freq):
    lines = line_freq.shape[0]
    columns = input_factor.shape[1] // lines
    half = columns // 2
    forced = lax.psum(
        lax.dot_general(
            input_rows, input_factor, (((0,), (0,)), ((), ())), preferred_element_type=F32
        ),
        AXES,
    )
    pieces = []
    for line in range(lines):
        gain_real, gain_imag = modal_gain(mode_freq, mode_damping, line_freq[line])
        gain_real, gain_imag = gain_real[:, None], gain_imag[:, None]
        real = forced[:, line * columns : line * columns + half]
        imag = forced[:, line * columns + half : (line + 1) * columns]
        pieces.append(gain_real * real - gain_imag * imag)
        pieces.append(gain_real * imag + gain_imag * real)
    return jnp.concatenate(pieces, axis=1).astype(BF16)


def pseudo_by_exchange(devices, input_rows, input_factor, mode_freq, mode_damping, line_freq):
    rows, modes = input_rows.shape
    width = input_factor.shape[1]
    blocks = input_rows.reshape(rows, devices, modes // devices).transpose(1, 0, 2)
    factors = jnp.broadcast_to(input_factor[None], (devices, rows, width))
    got = lax.all_to_all(jnp.concatenate([blocks, factors], axis=1), AXES, 0, 0)
    part = pseudo_part(got, line_freq, mode_freq, mode_damping, rows)
    return lax.all_gather(part, AXES, axis=0, tiled=True)


def local(
    devices,
    mode_rows,
    input_rows,
    input_factor,
    mode_freq,
    mode_damping,
    line_freq,
    boundary_rows,
    connectivity,
    stress_coef,
):
    rows, modes = input_rows.shape
    rim = boundary_rows.shape[0] // 2
    exports, high, low = setup(boundary_rows, connectivity, stress_coef, mode_rows)
    up = [(i, i + 1) for i in range(devices - 1)]
    down = [(i + 1, i) for i in range(devices - 1)]
    lower = lax.ppermute(exports[rim:], AXES, up)
    upper = lax.ppermute(exports[:rim], AXES, down)
    if modes == devices * LANES and input_factor.shape[1] == LANES and rows % 16 == 0:
        pseudo = pseudo_by_exchange(
            devices, input_rows, input_factor, mode_freq, mode_damping, line_freq
        )
    else:
        pseudo = pseudo_by_sum(input_rows, input_factor, mode_freq, mode_damping, line_freq)
    return stress_part(mode_rows, lower, upper, pseudo, high, low, line_freq.shape[0])


def solution(mesh):
    devices = 1
    for axis in AXES:
        devices *= mesh.shape[axis]
    placed = (
        P(AXES, None),
        P(AXES, None),
        P(AXES, None),
        P(),
        P(),
        P(),
        P(AXES),
        P(None, AXES),
        P(None, AXES),
    )
    return jax.shard_map(
        functools.partial(local, devices),
        mesh=mesh,
        in_specs=placed,
        out_specs=P(None, AXES),
        check_vma=False,
    )
```

time: 177 us -> 95.5 us (0.54)
  the two profiles are of different devices: /device:TPU:8 before, /device:TPU:0 now
where the time goes in v1:
time: 95.5 us; the launch traced here: 95 us
  waiting for transfers between devices  42.7 us (45%)
  blocking collectives  17.7 us (19%)
  between operations  13.5 us (14%)
  local copies, waits for them, and re-layouts  11.6 us (12%)
  Pallas kernels  6.42 us (7%)
  starting transfers between devices  3.14 us (3%)
    all_gather x1, waiting for transfers between devices, pseudo_by_exchange(): return lax.all_gather(part, AXES, axis=0, tiled=True)  40.2 us
    all_to_all x1, blocking collectives, pseudo_by_exchange(): got = lax.all_to_all(jnp.concatenate([blocks, factors], axis=1), AXES, 0, 0)  17.7 us
    unnamed x18, local copies, waits for them, and re-layouts  9.98 us
    pallas_call x1, Pallas kernels, stress_part(): pl.pallas_call(functools.partial(stress_kernel, lines=lines), out_shape=j...  3.57 us
    ppermute x1, waiting for transfers between devices, local(): upper = lax.ppermute(exports[:rim], AXES, down)  2.32 us
  transfers between devices with their start and end apart: 3, of which 3 were waited for; matrix products, arithmetic and copies ran while one was open for 1% of the time, Pallas kernels for 1%

profile of v1, /device:TPU:0, one launch (start us, length us, event | category | flops | bytes accessed | tf_op | source)
XLA Modules:
  0.0 95.0 jit_solution(408460729558313679)
XLA Ops:
  6.5 0.0 copy-start
  6.5 0.0 all-gather.2.cloned.1.call-start
  6.5 0.9 copy-done
  7.5 0.7 broadcast_in_dim.2
  8.2 17.7 %all_to_all.5.got_ref = bf16[32,32,128]{2,1,0:T(8,128)(2,1)S(1)} all-to-all(bf16[32,32,128]{2,1,0:T(8,128)(2,1)S(1)} %pad_maximum_fusion), channel_id=1, replica_groups=mesh['region'=8,'sub'=4] {'region','sub'}, dimensions={0} | all-to-all | bytes 524288 | tf_op jit(solution)/shard_map/all_to_all | solution.py:205
  25.9 0.0 copy-start.4
  25.9 0.7 copy-done.4
  26.6 0.0 copy-start.5
  26.6 0.7 copy-done.5
  27.3 0.0 copy-start.8
  27.3 0.7 copy-done.8
  28.0 1.4 %pseudo.1 = bf16[128,128]{1,0:T(8,128)(2,1)} custom-call(f32[2]{0:T(128)S(1)} %copy-done.8, f32[32,128]{1,0:T(8,128)S(1)} %bitcast.10, f32[32,128]{1,0:T(8,128)S(1)} %bitcast.11, bf16[32,32,128]{2,1,0:T(8,128)(2,1)S(1)} %all_to_all.5.got_ref), custom_call_target="tpu_custom_call" | custom-call | flops 16777216 | bytes 262144 | tf_op jit(solution)/shard_map/pseudo/pallas_call | solution.py:134
  29.4 0.0 all-gather.2.cloned.1.call-update
  29.5 0.8 copy.11.boundary_ref
  30.2 0.0 copy-start.1
  30.2 2.2 %copy-done.1 = bf16[512,4096]{1,0:T(8,128)(2,1)S(1)} copy-done((bf16[512,4096]{1,0:T(8,128)(2,1)S(1)}, bf16[512,4096]{1,0:T(8,128)(2,1)}, u32[]{:S(2)}) %copy-start.1) | copy-done | bytes 4194328
  32.4 0.0 copy-start.6
  32.4 0.7 copy-done.6
  33.1 0.0 copy-start.7
  33.1 0.7 copy-done.7
  33.8 1.4 %setup.1 = (bf16[128,4096]{1,0:T(8,128)(2,1)S(1)}, bf16[640,512]{1,0:T(8,128)(2,1)S(1)}, bf16[640,512]{1,0:T(8,128)(2,1)S(1)}) custom-call(s32[128,1]{1,0:T(8,128)S(1)} %copy.11.boundary_ref, s32[4,512]{1,0:T(4,128)S(1)} %copy-done.6, f32[4,512]{1,0:T(4,128)S(1)} %copy-done.7, bf16[512,4096]{1,0:T(8,128)(2,1)S(1)} %copy-done.1), custom_call_target="tpu_custom_call" | custom-call | flops 539492352 | bytes 6553600 | tf_op jit(solution)/shard_map/setup/pallas_call | solution.py:112
  35.2 0.1 fusion
  35.3 1.9 %collective-permute-start = (bf16[64,4096]{1,0:T(8,128)(2,1)S(1)}, bf16[64,4096]{1,0:T(8,128)(2,1)S(1)}, u32[]{:S(2)}, u32[]{:S(2)}) collective-permute-start(bf16[64,4096]{1,0:T(8,128)(2,1)S(1)} %get-tuple-element.12), channel_id=1, source_target_pairs={{0,1},{1,2},{2,3},{3,4},{4,5},{5,6},{6,7},{7,8},{8,9},{9,10},{10,1... | collective-permute-start | bytes 1572872 | tf_op jit(solution)/shard_map/ppermute | solution.py:227
  37.2 1.3 %collective-permute-start.1 = (bf16[64,4096]{1,0:T(8,128)(2,1)S(1)}, bf16[64,4096]{1,0:T(8,128)(2,1)S(1)}, u32[]{:S(2)}, u32[]{:S(2)}) collective-permute-start(bf16[64,4096]{1,0:T(8,128)(2,1)S(1)} %get-tuple-element.11), channel_id=1, source_target_pairs={{1,0},{2,1},{3,2},{4,3},{5,4},{6,5},{7,6},{8,7},{9,8},{10,9},{11,1... | collective-permute-start | bytes 1572872 | tf_op jit(solution)/shard_map/ppermute | solution.py:228
  38.5 0.2 collective-permute-done.lower_ref
  38.7 2.3 %collective-permute-done.1.upper_ref = bf16[64,4096]{1,0:T(8,128)(2,1)S(1)} collective-permute-done((bf16[64,4096]{1,0:T(8,128)(2,1)S(1)}, bf16[64,4096]{1,0:T(8,128)(2,1)S(1)}, u32[]{:S(2)}, u32[]{:S(2)}) %collective-permute-start.1) | collective-permute-done | bytes 524320 | tf_op jit(solution)/shard_map/ppermute | solution.py:228
  41.0 40.2 %all-gather.2.cloned.1.call-done.pseudo_ref = bf16[4096,128]{1,0:T(8,128)(2,1)} async-done(((bf16[128,128]{1,0:T(8,128)(2,1)}), bf16[4096,128]{1,0:T(8,128)(2,1)}) %all-gather.2.cloned.1.call-update) | async-done | bytes 1048592 | tf_op jit(solution)/shard_map/all_gather | solution.py:207
  81.1 0.0 copy-start.2
  81.2 2.2 %copy-done.2 = bf16[512,4096]{1,0:T(8,128)(2,1)S(1)} copy-done((bf16[512,4096]{1,0:T(8,128)(2,1)S(1)}, bf16[512,4096]{1,0:T(8,128)(2,1)}, u32[]{:S(2)}) %copy-start.2) | copy-done | bytes 4194328
  83.3 0.0 copy-start.3
  83.3 1.2 %copy-done.3 = bf16[4096,128]{1,0:T(8,128)(2,1)S(1)} copy-done((bf16[4096,128]{1,0:T(8,128)(2,1)S(1)}, bf16[4096,128]{1,0:T(8,128)(2,1)}, u32[]{:S(2)}) %copy-start.3) | copy-done | bytes 1048600
  84.6 3.6 %stress.1 = f32[2,512]{1,0:T(2,128)} custom-call(bf16[512,4096]{1,0:T(8,128)(2,1)S(1)} %copy-done.2, bf16[64,4096]{1,0:T(8,128)(2,1)S(1)} %collective-permute-done.lower_ref, bf16[64,4096]{1,0:T(8,128)(2,1)S(1)} %collective-permute-done.1.upper_ref, bf16[4096,128]{1,0:T(8,128)(2,1)S(1)} %copy-done.3, bf16[640,512]{1,0:T(8,128)(2,1)S(1)} %get-tuple-element.9.high_ref, ...), custom_call_target="tpu_custom_call" | custom-call | flops 838860800 | bytes 7602176 | tf_op jit(solution)/shard_map/stress/pallas_call | solution.py:155
  (2 shorter events, 0.0 us)
Async XLA Ops:
  6.5 0.9 copy-start
  6.5 74.6 %all-gather.2.cloned.1.call-start = ((), (), s32[]{:S(2)}) async-start(), calls=%async_computation.1 | async-start | bytes 1081344 | tf_op jit(solution)/shard_map/all_gather | solution.py:207
  25.9 0.7 copy-start.4
  26.6 0.7 copy-start.5
  27.3 0.7 copy-start.8
  30.2 2.2 %copy-start.1 = (bf16[512,4096]{1,0:T(8,128)(2,1)S(1)}, bf16[512,4096]{1,0:T(8,128)(2,1)}, u32[]{:S(2)}) copy-start(bf16[512,4096]{1,0:T(8,128)(2,1)} %own_ref.1) | copy-start | bytes 12582916
  32.4 0.7 copy-start.6
  33.1 0.7 copy-start.7
  35.3 3.3 %collective-permute-start = (bf16[64,4096]{1,0:T(8,128)(2,1)S(1)}, bf16[64,4096]{1,0:T(8,128)(2,1)S(1)}, u32[]{:S(2)}, u32[]{:S(2)}) collective-permute-start(bf16[64,4096]{1,0:T(8,128)(2,1)S(1)} %get-tuple-element.12), channel_id=1, source_target_pairs={{0,1},{1,2},{2,3},{3,4},{4,5},{5,6},{6,7},{7,8},{8,9},{9,10},{10,1... | collective-permute-start | bytes 1572872 | tf_op jit(solution)/shard_map/ppermute | solution.py:227
  37.2 3.8 %collective-permute-start.1 = (bf16[64,4096]{1,0:T(8,128)(2,1)S(1)}, bf16[64,4096]{1,0:T(8,128)(2,1)S(1)}, u32[]{:S(2)}, u32[]{:S(2)}) collective-permute-start(bf16[64,4096]{1,0:T(8,128)(2,1)S(1)} %get-tuple-element.11), channel_id=1, source_target_pairs={{1,0},{2,1},{3,2},{4,3},{5,4},{6,5},{7,6},{8,7},{9,8},{10,9},{11,1... | collective-permute-start | bytes 1572872 | tf_op jit(solution)/shard_map/ppermute | solution.py:228
  81.1 2.2 %copy-start.2 = (bf16[512,4096]{1,0:T(8,128)(2,1)S(1)}, bf16[512,4096]{1,0:T(8,128)(2,1)}, u32[]{:S(2)}) copy-start(bf16[512,4096]{1,0:T(8,128)(2,1)} %own_ref.1) | copy-start | bytes 12582916
  83.3 1.2 %copy-start.3 = (bf16[4096,128]{1,0:T(8,128)(2,1)S(1)}, bf16[4096,128]{1,0:T(8,128)(2,1)}, u32[]{:S(2)}) copy-start(bf16[4096,128]{1,0:T(8,128)(2,1)} %all-gather.2.cloned.1.call-done.pseudo_ref) | copy-start | bytes 3145732
Sparse Core Ops, SparseCore 0:
  29.6 51.5 all-gather.1

commit v2 on v1

v2 whole, which is shorter than its diff:
```python
import functools
import math

import jax
import jax.numpy as jnp
from jax import lax
from jax.experimental import pallas as pl
from jax.experimental.pallas import tpu as pltpu
from jax.sharding import PartitionSpec as P

AXES = ("region", "sub")
LANES = 128
F32 = jnp.float32
BF16 = jnp.bfloat16
VMEM_BYTES = 24 * 1024 * 1024
FAST_SHAPE = (8, 4)


def whole(*_):
    return pl.BlockSpec(memory_space=pltpu.VMEM)


def modal_gain(freq, damping, omega):
    detune = freq * freq - omega * omega
    damped = 2.0 * damping * freq * omega
    magnitude = detune * detune + damped * damped
    return detune / magnitude, -damped / magnitude


def setup_kernel(connect_ref, coef_ref, high_ref, low_ref):
    nodes, elems = high_ref.shape
    tall = 64
    for start in range(0, nodes, tall):
        node = lax.broadcasted_iota(jnp.int32, (tall, elems), 0) + start
        total = jnp.zeros((tall, elems), F32)
        for corner in range(connect_ref.shape[0]):
            hit = node == connect_ref[corner : corner + 1, :]
            total = total + jnp.where(hit, coef_ref[corner : corner + 1, :], 0.0)
        high = total.astype(BF16)
        high_ref[start : start + tall, :] = high
        low_ref[start : start + tall, :] = (total - high.astype(F32)).astype(BF16)


def scale_transposed(forced, freq, damping, line_ref, columns):
    half = columns // 2
    pieces = []
    for line in range(line_ref.shape[0]):
        gain_real, gain_imag = modal_gain(freq, damping, line_ref[line])
        real = forced[line * columns : line * columns + half]
        imag = forced[line * columns + half : (line + 1) * columns]
        pieces.append(gain_real * real - gain_imag * imag)
        pieces.append(gain_real * imag + gain_imag * real)
    return jnp.concatenate(pieces, axis=0)


def slab_of(device):
    core = device % 2
    plane = (device // 2) % 4
    return core * 16 + plane * 4 + device // 8


def pseudo_kernel(line_ref, freq_ref, damping_ref, got_ref, pseudo_ref, *, rows):
    devices, _, width = got_ref.shape
    slab = slab_of(lax.axis_index(AXES))
    shapes = got_ref[:, :rows, :].reshape(devices * rows, width)
    factor = got_ref[:, rows:, :].reshape(devices * rows, width)
    forced = lax.dot_general(
        factor, shapes, (((0,), (0,)), ((), ())), preferred_element_type=F32
    )
    columns = width // line_ref.shape[0]
    scaled = scale_transposed(
        forced, freq_ref[pl.ds(slab, 1), :], damping_ref[pl.ds(slab, 1), :], line_ref, columns
    )
    pseudo_ref[...] = scaled.T.astype(BF16)


def first_kernel(modes_ref, pseudo_ref, total_ref):
    depth = pseudo_ref.shape[0]
    core = lax.axis_index(AXES) % 2
    here = pl.ds(pl.multiple_of(core * depth, depth), depth)
    total_ref[...] = jnp.dot(modes_ref[:, here], pseudo_ref[...], preferred_element_type=F32)


def second_kernel(boundary_ref, modes_ref, pseudo_ref, total_ref, table_ref, export_ref):
    rows = modes_ref.shape[0]
    depth = pseudo_ref.shape[0]
    exports = export_ref.shape[0]
    other = 1 - lax.axis_index(AXES) % 2
    here = pl.ds(pl.multiple_of(other * depth, depth), depth)
    total = total_ref[...] + jnp.dot(
        modes_ref[:, here], pseudo_ref[...], preferred_element_type=F32
    )
    responses = total.astype(BF16)
    pick = lax.broadcasted_iota(jnp.int32, (exports, rows), 1) == boundary_ref[...]
    pick = pick.astype(F32).astype(BF16)
    export_ref[...] = jnp.dot(pick, responses, preferred_element_type=F32).astype(BF16)
    table_ref[...] = total.T.astype(BF16)


def own_kernel(table_ref, high_ref, low_ref, stress_ref, *, rim):
    rows = table_ref.shape[1]
    table = table_ref[...]
    stress = jnp.dot(table, high_ref[rim : rim + rows, :], preferred_element_type=F32)
    stress_ref[...] = stress + jnp.dot(
        table, low_ref[rim : rim + rows, :], preferred_element_type=F32
    )


def power_kernel(stress_ref, lower_ref, upper_ref, high_ref, low_ref, power_ref):
    rim = lower_ref.shape[0]
    nodes = high_ref.shape[0]
    lines = power_ref.shape[0]
    stress = stress_ref[...]
    for rows_ref, start in ((lower_ref, 0), (upper_ref, nodes - rim)):
        for part in (high_ref, low_ref):
            stress = stress + lax.dot_general(
                rows_ref[...],
                part[start : start + rim, :],
                (((0,), (0,)), ((), ())),
                preferred_element_type=F32,
            )
    squares = stress * stress
    columns = squares.shape[0] // lines
    for line in range(lines):
        power_ref[line : line + 1, :] = (
            jnp.sum(squares[line * columns : (line + 1) * columns], axis=0, keepdims=True)
            / columns
        )


def call(kernel, name, out, *operands, flops, smem=0):
    shapes = [jax.ShapeDtypeStruct(shape, dtype) for shape, dtype in out]
    moved = sum(x.size * x.dtype.itemsize for x in operands)
    moved += sum(math.prod(shape) * jnp.dtype(dtype).itemsize for shape, dtype in out)
    specs = [pl.BlockSpec(memory_space=pltpu.SMEM)] * smem + [whole()] * (len(operands) - smem)
    result = pl.pallas_call(
        kernel,
        out_shape=shapes,
        in_specs=specs,
        out_specs=[whole()] * len(out),
        compiler_params=pltpu.CompilerParams(vmem_limit_bytes=VMEM_BYTES),
        cost_estimate=pl.CostEstimate(flops=flops, bytes_accessed=moved, transcendentals=0),
        name=name,
    )(*operands)
    return result if len(out) > 1 else result[0]


def pseudo_by_sum(input_rows, input_factor, mode_freq, mode_damping, line_freq):
    lines = line_freq.shape[0]
    columns = input_factor.shape[1] // lines
    half = columns // 2
    forced = lax.psum(
        lax.dot_general(
            input_rows, input_factor, (((0,), (0,)), ((), ())), preferred_element_type=F32
        ),
        AXES,
    )
    pieces = []
    for line in range(lines):
        gain_real, gain_imag = modal_gain(mode_freq, mode_damping, line_freq[line])
        gain_real, gain_imag = gain_real[:, None], gain_imag[:, None]
        real = forced[:, line * columns : line * columns + half]
        imag = forced[:, line * columns + half : (line + 1) * columns]
        pieces.append(gain_real * real - gain_imag * imag)
        pieces.append(gain_real * imag + gain_imag * real)
    return jnp.concatenate(pieces, axis=1).astype(BF16)


def gather_by(block, groups):
    count = len(groups[0])
    sent = jnp.broadcast_to(block[None], (count,) + block.shape)
    got = lax.all_to_all(sent, AXES, 0, 0, axis_index_groups=groups)
    return got.reshape((count * block.shape[0],) + block.shape[1:])


def own_pseudo(input_rows, input_factor, mode_freq, mode_damping, line_freq):
    devices = math.prod(FAST_SHAPE)
    rows, modes = input_rows.shape
    width = input_factor.shape[1]
    slab = modes // devices
    blocks = input_rows.reshape(rows, 2, 4, 4, slab).transpose(3, 2, 1, 0, 4)
    blocks = blocks.reshape(devices, rows, slab)
    factors = jnp.broadcast_to(input_factor[None], (devices, rows, width))
    got = lax.all_to_all(jnp.concatenate([blocks, factors], axis=1), AXES, 0, 0)
    return call(
        functools.partial(pseudo_kernel, rows=rows),
        "pseudo",
        [((slab, width), BF16)],
        line_freq,
        mode_freq.reshape(devices, slab),
        mode_damping.reshape(devices, slab),
        got,
        flops=2 * devices * rows * slab * width,
        smem=1,
    )


def local(
    shape,
    mode_rows,
    input_rows,
    input_factor,
    mode_freq,
    mode_damping,
    line_freq,
    boundary_rows,
    connectivity,
    stress_coef,
):
    devices = math.prod(shape)
    rows, modes = mode_rows.shape
    width = input_factor.shape[1]
    lines = line_freq.shape[0]
    exports = boundary_rows.shape[0]
    rim = exports // 2
    elems = connectivity.shape[1]
    nodes = rows + exports
    high, low = call(
        setup_kernel,
        "setup",
        [((nodes, elems), BF16)] * 2,
        connectivity,
        stress_coef,
        flops=16 * nodes * elems,
    )
    inputs = (input_rows, input_factor, mode_freq, mode_damping, line_freq)
    if shape == FAST_SHAPE and modes == devices * LANES and input_rows.shape[0] % 16 == 0:
        block = own_pseudo(*inputs)
        columns = [[z * 8 + plane for z in range(4)] for plane in range(8)]
        planes = [[z * 8 + p * 2 + c for p in range(4)] for z in range(4) for c in range(2)]
        mine = gather_by(gather_by(block, columns), planes)
        theirs = lax.ppermute(mine, AXES, [(i, i ^ 1) for i in range(devices)])
    else:
        pseudo = pseudo_by_sum(*inputs).reshape(2, modes // 2, width)
        core = lax.axis_index(AXES) % 2
        mine = lax.dynamic_index_in_dim(pseudo, core, 0, keepdims=False)
        theirs = lax.dynamic_index_in_dim(pseudo, 1 - core, 0, keepdims=False)
    total = call(
        first_kernel,
        "first",
        [((rows, width), F32)],
        mode_rows,
        mine,
        flops=rows * modes * width,
    )
    table, export = call(
        second_kernel,
        "second",
        [((width, rows), BF16), ((exports, width), BF16)],
        boundary_rows.reshape(exports, 1),
        mode_rows,
        theirs,
        total,
        flops=rows * modes * width + 2 * exports * rows * width,
    )
    lower = lax.ppermute(export[rim:], AXES, [(i, i + 1) for i in range(devices - 1)])
    upper = lax.ppermute(export[:rim], AXES, [(i + 1, i) for i in range(devices - 1)])
    stress = call(
        functools.partial(own_kernel, rim=rim),
        "own",
        [((width, elems), F32)],
        table,
        high,
        low,
        flops=4 * rows * elems * width,
    )
    return call(
        power_kernel,
        "power",
        [((lines, elems), F32)],
        stress,
        lower,
        upper,
        high,
        low,
        flops=4 * exports * elems * width,
    )


def solution(mesh):
    shape = tuple(mesh.shape[axis] for axis in AXES)
    placed = (
        P(AXES, None),
        P(AXES, None),
        P(AXES, None),
        P(),
        P(),
        P(),
        P(AXES),
        P(None, AXES),
        P(None, AXES),
    )
    return jax.shard_map(
        functools.partial(local, shape),
        mesh=mesh,
        in_specs=placed,
        out_specs=P(None, AXES),
        check_vma=False,
    )
```

time: 95.5 us -> 55.1 us (0.58)
  the two profiles are of different devices: /device:TPU:0 before, /device:TPU:8 now
where the time goes in v2:
time: 55.1 us; the launch traced here: 54.7 us
  blocking collectives  34.4 us (62%)
  local copies, waits for them, and re-layouts  6.87 us (12%)
  starting transfers between devices  5.06 us (9%)
  Pallas kernels  4.29 us (8%)
  waiting for transfers between devices  3.94 us (7%)
    all_to_all x2, blocking collectives, gather_by(): got = lax.all_to_all(sent, AXES, 0, 0, axis_index_groups=groups)  18.8 us
    all_to_all x1, blocking collectives, own_pseudo(): got = lax.all_to_all(jnp.concatenate([blocks, factors], axis=1), AXES, 0, 0)  15.6 us
    pallas_call x6, Pallas kernels, call(): pl.pallas_call(kernel, out_shape=shapes, in_specs=specs, out_specs=[whole...  4.29 us
    unnamed x12, local copies, waits for them, and re-layouts  4.28 us
    ppermute x1, waiting for transfers between devices, local(): lax.ppermute(export[rim:], AXES, [(i, i + 1) for i in range(devices - 1)])  3.93 us
    ppermute x1, starting transfers between devices, local(): lax.ppermute(export[:rim], AXES, [(i + 1, i) for i in range(devices - 1)])  3.14 us
    ppermute x1, starting transfers between devices, local(): lax.ppermute(export[rim:], AXES, [(i, i + 1) for i in range(devices - 1)])  1.92 us
  transfers between devices with their start and end apart: 3, of which 1 were waited for; matrix products, arithmetic and copies ran while one was open for 1% of the time, Pallas kernels for 3%

profile of v2, /device:TPU:8, one launch (start us, length us, event | category | flops | bytes accessed | tf_op | source)
XLA Modules:
  0.0 54.7 jit_solution(7751842252311404372)
XLA Ops:
  0.0 1.0 %reshape.24 = bf16[16,2,4,4,128]{4,3,2,1,0:T(4,128)(2,1)S(1)} reshape(bf16[16,4096]{1,0:T(8,128)(2,1)} %param.10) | data formatting | bytes 262144 | tf_op jit(solution)/shard_map/reshape | solution.py:181
  1.0 0.1 copy.10
  1.0 0.7 %broadcast_in_dim.8 = bf16[32,16,128]{2,1,0:T(8,128)(2,1)S(1)} broadcast(bf16[16,128]{1,0:T(8,128)(2,1)} %param.11), dimensions={1,2} | broadcast | bytes 135168 | tf_op jit(solution)/shard_map/broadcast_in_dim | solution.py:183
  1.8 15.6 %all_to_all.15.got_ref = bf16[32,32,128]{2,1,0:T(8,128)(2,1)S(1)} all-to-all(bf16[32,32,128]{2,1,0:T(8,128)(2,1)S(1)} %pad_maximum_fusion), channel_id=1, replica_groups=mesh['region'=8,'sub'=4] {'region','sub'}, dimensions={0} | all-to-all | bytes 524288 | tf_op jit(solution)/shard_map/all_to_all | solution.py:184
  17.4 0.0 copy-start.1
  17.4 0.7 %copy-done.1 = f32[4096]{0:T(1024)S(1)} copy-done((f32[4096]{0:T(1024)S(1)}, f32[4096]{0:T(1024)}, u32[]{:S(2)}) %copy-start.1) | copy-done | bytes 16408
  18.1 0.0 copy-start.2
  18.1 0.7 %copy-done.2 = f32[4096]{0:T(1024)S(1)} copy-done((f32[4096]{0:T(1024)S(1)}, f32[4096]{0:T(1024)}, u32[]{:S(2)}) %copy-start.2) | copy-done | bytes 16408
  18.8 0.0 copy-start.3
  18.8 0.7 %copy-done.3 = f32[2]{0:T(128)S(1)} copy-done((f32[2]{0:T(128)S(1)}, f32[2]{0:T(128)}, u32[]{:S(2)}) %copy-start.3) | copy-done | bytes 32
  19.5 0.8 %pseudo.1 = bf16[128,128]{1,0:T(8,128)(2,1)S(1)} custom-call(f32[2]{0:T(128)S(1)} %copy-done.3, f32[32,128]{1,0:T(8,128)S(1)} %bitcast.10, f32[32,128]{1,0:T(8,128)S(1)} %bitcast.11, bf16[32,32,128]{2,1,0:T(8,128)(2,1)S(1)} %all_to_all.15.got_ref), custom_call_target="tpu_custom_call" | custom-call | flops 16777216 | bytes 327688 | tf_op jit(solution)/shard_map/pseudo/pallas_call | solution.py:136
  20.3 8.7 %all_to_all.16 = bf16[4,128,128]{2,1,0:T(8,128)(2,1)S(1)} all-to-all(bf16[4,128,128]{2,1,0:T(8,128)(2,1)S(1)} %broadcast_in_dim.9), channel_id=1, replica_groups={{0,8,16,24},{1,9,17,25},{2,10,18,26},{3,11,19,27},{4,12,20,28},{5,13,21..., dimensions={0} | all-to-all | bytes 262144 | tf_op jit(solution)/shard_map/all_to_all | solution.py:172
  29.0 0.1 broadcast_in_dim.22
  29.1 10.1 %all_to_all.17 = bf16[4,512,128]{2,1,0:T(8,128)(2,1)S(1)} all-to-all(bf16[4,512,128]{2,1,0:T(8,128)(2,1)S(1)} %broadcast_in_dim.22), channel_id=1, replica_groups={{0,2,4,6},{1,3,5,7},{8,10,12,14},{9,11,13,15},{16,18,20,22},{17,19,21,2..., dimensions={0} | all-to-all | bytes 1048576 | tf_op jit(solution)/shard_map/all_to_all | solution.py:172
  39.2 0.0 collective-permute-start
  39.2 0.8 %copy.11.boundary_ref = s32[128,1]{1,0:T(8,128)S(1)} copy(s32[128,1]{0,1:T(1,128)} %bitcast.14) | data formatting | bytes 1024 | tf_op jit(solution)/shard_map/reshape | solution.py:250
  40.0 0.0 copy-start
  40.0 2.2 %copy-done = bf16[512,4096]{1,0:T(8,128)(2,1)S(1)} copy-done((bf16[512,4096]{1,0:T(8,128)(2,1)S(1)}, bf16[512,4096]{1,0:T(8,128)(2,1)}, u32[]{:S(2)}) %copy-start) | copy-done | bytes 4194328
  42.1 0.0 copy-start.4
  42.1 0.0 copy-start.5
  42.2 0.7 %first.1.total_ref = f32[512,128]{1,0:T(8,128)S(1)} custom-call(bf16[512,4096]{1,0:T(8,128)(2,1)S(1)} %copy-done, bf16[2048,128]{1,0:T(8,128)(2,1)S(1)} %bitcast.9), custom_call_target="tpu_custom_call" | custom-call | flops 268435456 | bytes 4980736 | tf_op jit(solution)/shard_map/first/pallas_call | solution.py:136
  42.9 0.0 collective-permute-done.pseudo_ref
  42.9 0.9 %second.1 = (bf16[128,512]{1,0:T(8,128)(2,1)S(1)}, bf16[128,128]{1,0:T(8,128)(2,1)S(1)}) custom-call(s32[128,1]{1,0:T(8,128)S(1)} %copy.11.boundary_ref, bf16[512,4096]{1,0:T(8,128)(2,1)S(1)} %copy-done, bf16[2048,128]{1,0:T(8,128)(2,1)S(1)} %collective-permute-done.pseudo_ref, f32[512,128]{1,0:T(8,128)S(1)} %first.1.total_ref), custom_call_target="tpu_custom_call" | custom-call | flops 285212672 | bytes 5145088 | tf_op jit(solution)/shard_map/second/pallas_call | solution.py:136
  43.8 3.1 %collective-permute-start.2 = (bf16[64,128]{1,0:T(8,128)(2,1)S(1)}, bf16[64,128]{1,0:T(8,128)(2,1)S(1)}, u32[]{:S(2)}, u32[]{:S(2)}) collective-permute-start(bf16[64,128]{1,0:T(8,128)(2,1)S(1)} %get-tuple-element.13), channel_id=1, source_target_pairs={{1,0},{2,1},{3,2},{4,3},{5,4},{6,5},{7,6},{8,7},{9,8},{10,9},{11,1... | collective-permute-start | bytes 49160 | tf_op jit(solution)/shard_map/ppermute | solution.py:257
  46.9 1.9 %collective-permute-start.1 = (bf16[64,128]{1,0:T(8,128)(2,1)S(1)}, bf16[64,128]{1,0:T(8,128)(2,1)S(1)}, u32[]{:S(2)}, u32[]{:S(2)}) collective-permute-start(bf16[64,128]{1,0:T(8,128)(2,1)S(1)} %get-tuple-element.14), channel_id=1, source_target_pairs={{0,1},{1,2},{2,3},{3,4},{4,5},{5,6},{6,7},{7,8},{8,9},{9,10},{10,1... | collective-permute-start | bytes 49160 | tf_op jit(solution)/shard_map/ppermute | solution.py:256
  48.8 0.0 copy-done.4
  48.8 0.0 copy-done.5
  48.9 0.6 %setup.1 = (bf16[640,512]{1,0:T(8,128)(2,1)S(1)}, bf16[640,512]{1,0:T(8,128)(2,1)S(1)}) custom-call(s32[4,512]{1,0:T(4,128)S(1)} %copy-done.4, f32[4,512]{1,0:T(4,128)S(1)} %copy-done.5), custom_call_target="tpu_custom_call" | custom-call | flops 5242880 | bytes 1327104 | tf_op jit(solution)/shard_map/setup/pallas_call | solution.py:136
  49.5 0.3 own.1.stress_ref
  49.8 0.0 collective-permute-done.2.upper_ref
  49.8 3.9 %collective-permute-done.1.lower_ref = bf16[64,128]{1,0:T(8,128)(2,1)S(1)} collective-permute-done((bf16[64,128]{1,0:T(8,128)(2,1)S(1)}, bf16[64,128]{1,0:T(8,128)(2,1)S(1)}, u32[]{:S(2)}, u32[]{:S(2)}) %collective-permute-start.1) | collective-permute-done | bytes 16416 | tf_op jit(solution)/shard_map/ppermute | solution.py:256
  53.8 0.9 %power.1 = f32[2,512]{1,0:T(2,128)} custom-call(f32[128,512]{1,0:T(8,128)S(1)} %own.1.stress_ref, bf16[64,128]{1,0:T(8,128)(2,1)S(1)} %collective-permute-done.1.lower_ref, bf16[64,128]{1,0:T(8,128)(2,1)S(1)} %collective-permute-done.2.upper_ref, bf16[640,512]{1,0:T(8,128)(2,1)S(1)} %get-tuple-element.10.high_ref, bf16[640,512]{1,0:T(8,128)(2,1)S(1)} %get-tuple-element.11.low_ref), custom_call_target="tpu_custom_call" | custom-call | flops 33554432 | bytes 1609728 | tf_op jit(solution)/shard_map/power/pallas_call | solution.py:136
  (3 shorter events, 0.0 us)
Async XLA Ops:
  17.4 0.7 %copy-start.1 = (f32[4096]{0:T(1024)S(1)}, f32[4096]{0:T(1024)}, u32[]{:S(2)}) copy-start(f32[4096]{0:T(1024)} %param.12) | copy-start | bytes 49156
  18.1 0.7 %copy-start.2 = (f32[4096]{0:T(1024)S(1)}, f32[4096]{0:T(1024)}, u32[]{:S(2)}) copy-start(f32[4096]{0:T(1024)} %param.13) | copy-start | bytes 49156
  18.8 0.7 %copy-start.3 = (f32[2]{0:T(128)S(1)}, f32[2]{0:T(128)}, u32[]{:S(2)}) copy-start(f32[2]{0:T(128)} %line_ref.1) | copy-start | bytes 28
  39.2 3.7 %collective-permute-start = (bf16[2048,128]{1,0:T(8,128)(2,1)S(1)}, bf16[2048,128]{1,0:T(8,128)(2,1)S(1)}, u32[]{:S(2)}, u32[]{:S(2)}) collective-permute-start(bf16[2048,128]{1,0:T(8,128)(2,1)S(1)} %bitcast.8), channel_id=1, source_target_pairs={{0,1},{1,0},{2,3},{3,2},{4,5},{5,4},{6,7},{7,6},{8,9},{9,8},{10,11... | collective-permute-start | bytes 1572872 | tf_op jit(solution)/shard_map/ppermute | solution.py:232
  40.0 2.2 %copy-start = (bf16[512,4096]{1,0:T(8,128)(2,1)S(1)}, bf16[512,4096]{1,0:T(8,128)(2,1)}, u32[]{:S(2)}) copy-start(bf16[512,4096]{1,0:T(8,128)(2,1)} %modes_ref.3) | copy-start | bytes 12582916
  42.1 6.7 %copy-start.4 = (s32[4,512]{1,0:T(4,128)S(1)}, s32[4,512]{1,0:T(4,128)}, u32[]{:S(2)}) copy-start(s32[4,512]{1,0:T(4,128)} %connect_ref.1) | copy-start | bytes 24580
  42.1 6.7 %copy-start.5 = (f32[4,512]{1,0:T(4,128)S(1)}, f32[4,512]{1,0:T(4,128)}, u32[]{:S(2)}) copy-start(f32[4,512]{1,0:T(4,128)} %coef_ref.1) | copy-start | bytes 24580
  43.8 6.1 %collective-permute-start.2 = (bf16[64,128]{1,0:T(8,128)(2,1)S(1)}, bf16[64,128]{1,0:T(8,128)(2,1)S(1)}, u32[]{:S(2)}, u32[]{:S(2)}) collective-permute-start(bf16[64,128]{1,0:T(8,128)(2,1)S(1)} %get-tuple-element.13), channel_id=1, source_target_pairs={{1,0},{2,1},{3,2},{4,3},{5,4},{6,5},{7,6},{8,7},{9,8},{10,9},{11,1... | collective-permute-start | bytes 49160 | tf_op jit(solution)/shard_map/ppermute | solution.py:257
  46.9 6.9 %collective-permute-start.1 = (bf16[64,128]{1,0:T(8,128)(2,1)S(1)}, bf16[64,128]{1,0:T(8,128)(2,1)S(1)}, u32[]{:S(2)}, u32[]{:S(2)}) collective-permute-start(bf16[64,128]{1,0:T(8,128)(2,1)S(1)} %get-tuple-element.14), channel_id=1, source_target_pairs={{0,1},{1,2},{2,3},{3,4},{4,5},{5,6},{6,7},{7,8},{8,9},{9,10},{10,1... | collective-permute-start | bytes 49160 | tf_op jit(solution)/shard_map/ppermute | solution.py:256

commit v3 on v2

v3 whole, which is shorter than its diff:
```python
import functools
import math

import jax
import jax.numpy as jnp
from jax import lax
from jax.experimental import pallas as pl
from jax.experimental.pallas import tpu as pltpu
from jax.sharding import PartitionSpec as P

AXES = ("region", "sub")
LANES = 128
F32 = jnp.float32
BF16 = jnp.bfloat16
VMEM_BYTES = 24 * 1024 * 1024
VMEM_MOST = 50 * 1024 * 1024
VMEM_ALL = 60 * 1024 * 1024
FAST_SHAPE = (8, 4)


def whole(*_):
    return pl.BlockSpec(memory_space=pltpu.VMEM)


def remains():
    return pl.BlockSpec(memory_space=pltpu.HBM)


def modal_gain(freq, damping, omega):
    detune = freq * freq - omega * omega
    damped = 2.0 * damping * freq * omega
    magnitude = detune * detune + damped * damped
    return detune / magnitude, -damped / magnitude


def setup_kernel(connect_ref, coef_ref, high_ref, low_ref):
    nodes, elems = high_ref.shape
    tall = 64
    for start in range(0, nodes, tall):
        node = lax.broadcasted_iota(jnp.int32, (tall, elems), 0) + start
        total = jnp.zeros((tall, elems), F32)
        for corner in range(connect_ref.shape[0]):
            hit = node == connect_ref[corner : corner + 1, :]
            total = total + jnp.where(hit, coef_ref[corner : corner + 1, :], 0.0)
        high = total.astype(BF16)
        high_ref[start : start + tall, :] = high
        low_ref[start : start + tall, :] = (total - high.astype(F32)).astype(BF16)


def slab_of(device):
    core = device % 2
    plane = (device // 2) % 4
    return core * 16 + plane * 4 + device // 8


def pack_kernel(
    line_hbm, freq_hbm, damping_hbm, rows_hbm, factor_hbm, sent_ref, gain_ref,
    line_ref, freq_ref, damping_ref, rows_ref, factor_ref, sems,
):
    devices, _, width = sent_ref.shape
    rows = rows_ref.shape[0]
    pairs = (
        (rows_hbm, rows_ref),
        (factor_hbm, factor_ref),
        (line_hbm, line_ref),
        (freq_hbm, freq_ref),
        (damping_hbm, damping_ref),
    )
    copies = [pltpu.make_async_copy(a, b, sems.at[k]) for k, (a, b) in enumerate(pairs)]
    for copy in copies:
        copy.start()
    copies[0].wait()
    copies[1].wait()
    factor = factor_ref[...]
    for device in range(devices):
        slab = slab_of(device)
        sent_ref[device, :rows, :] = rows_ref[:, slab * width : (slab + 1) * width]
        sent_ref[device, rows:, :] = factor
    for copy in copies[2:]:
        copy.wait()
    slab = pl.ds(slab_of(lax.axis_index(AXES)), 1)
    for line in range(line_ref.shape[0]):
        real, imag = modal_gain(freq_ref[slab, :], damping_ref[slab, :], line_ref[line])
        gain_ref[2 * line : 2 * line + 1, :] = real
        gain_ref[2 * line + 1 : 2 * line + 2, :] = imag


def pseudo_kernel(gain_ref, got_ref, pseudo_ref, *, rows, lines):
    devices, _, width = got_ref.shape
    shapes = got_ref[:, :rows, :].reshape(devices * rows, width)
    factor = got_ref[:, rows:, :].reshape(devices * rows, width)
    forced = lax.dot_general(
        factor, shapes, (((0,), (0,)), ((), ())), preferred_element_type=F32
    )
    columns = width // lines
    half = columns // 2
    pieces = []
    for line in range(lines):
        gain_real = gain_ref[2 * line : 2 * line + 1, :]
        gain_imag = gain_ref[2 * line + 1 : 2 * line + 2, :]
        real = forced[line * columns : line * columns + half]
        imag = forced[line * columns + half : (line + 1) * columns]
        pieces.append(gain_real * real - gain_imag * imag)
        pieces.append(gain_real * imag + gain_imag * real)
    pseudo = jnp.concatenate(pieces, axis=0).T.astype(BF16)
    for copy in range(pseudo_ref.shape[0]):
        pseudo_ref[copy] = pseudo


def first_kernel(
    boundary_hbm, modes_hbm, pseudo_ref, total_ref, other_ref, pick_ref, boundary_ref, near_ref, sems
):
    depth = pseudo_ref.shape[0]
    parts = sems.shape[0] - 2
    step = depth // parts
    core = lax.axis_index(AXES) % 2
    copies = [
        pltpu.make_async_copy(
            modes_hbm.at[:, pl.ds(pl.multiple_of(core * depth + k * step, step), step)],
            near_ref.at[:, k * step : (k + 1) * step],
            sems.at[k],
        )
        for k in range(parts)
    ]
    copies.append(pltpu.make_async_copy(boundary_hbm, boundary_ref, sems.at[parts]))
    copies.append(
        pltpu.make_async_copy(
            modes_hbm.at[:, pl.ds(pl.multiple_of((1 - core) * depth, depth), depth)],
            other_ref,
            sems.at[parts + 1],
        )
    )
    for copy in copies:
        copy.start()
    total = None
    for k in range(parts):
        copies[k].wait()
        here = slice(k * step, (k + 1) * step)
        term = jnp.dot(near_ref[:, here], pseudo_ref[here, :], preferred_element_type=F32)
        total = term if total is None else total + term
    total_ref[...] = total
    copies[parts].wait()
    pick = lax.broadcasted_iota(jnp.int32, pick_ref.shape, 0) == boundary_ref[...]
    pick_ref[...] = pick.astype(F32).astype(BF16)
    copies[parts + 1].wait()


def second_kernel(pick_ref, modes_ref, pseudo_ref, total_ref, table_ref, far_ref, near_ref):
    total = total_ref[...] + jnp.dot(
        modes_ref[...], pseudo_ref[...], preferred_element_type=F32
    )
    export = lax.dot_general(
        pick_ref[...], total.astype(BF16), (((0,), (0,)), ((), ())), preferred_element_type=F32
    ).astype(BF16)
    odd = lax.axis_index(AXES) % 2 == 1
    rim = far_ref.shape[0]
    far_ref[...] = jnp.where(odd, export[rim:], export[:rim])
    near_ref[...] = jnp.where(odd, export[:rim], export[rim:])
    table_ref[...] = total.T.astype(BF16)


def own_kernel(table_ref, high_ref, low_ref, stress_ref, *, rim):
    rows = table_ref.shape[1]
    table = table_ref[...]
    stress = jnp.dot(table, high_ref[rim : rim + rows, :], preferred_element_type=F32)
    stress_ref[...] = stress + jnp.dot(
        table, low_ref[rim : rim + rows, :], preferred_element_type=F32
    )


def power_kernel(stress_ref, far_ref, near_ref, high_ref, low_ref, power_ref):
    rim = far_ref.shape[0]
    nodes = high_ref.shape[0]
    lines = power_ref.shape[0]
    odd = lax.axis_index(AXES) % 2
    after = nodes - rim
    stress = stress_ref[...]
    for rows_ref, start in ((near_ref, after * (1 - odd)), (far_ref, after * odd)):
        here = pl.ds(pl.multiple_of(start, rim), rim)
        for part in (high_ref, low_ref):
            stress = stress + lax.dot_general(
                rows_ref[...],
                part[here, :],
                (((0,), (0,)), ((), ())),
                preferred_element_type=F32,
            )
    squares = stress * stress
    columns = squares.shape[0] // lines
    for line in range(lines):
        power_ref[line : line + 1, :] = (
            jnp.sum(squares[line * columns : (line + 1) * columns], axis=0, keepdims=True)
            / columns
        )


def call(kernel, name, out, *operands, flops, hbm=0, scratch=(), vmem=VMEM_BYTES):
    shapes = [jax.ShapeDtypeStruct(shape, dtype) for shape, dtype in out]
    moved = sum(x.size * x.dtype.itemsize for x in operands)
    moved += sum(math.prod(shape) * jnp.dtype(dtype).itemsize for shape, dtype in out)
    result = pl.pallas_call(
        kernel,
        out_shape=shapes,
        in_specs=[remains()] * hbm + [whole()] * (len(operands) - hbm),
        out_specs=[whole()] * len(out),
        scratch_shapes=scratch,
        compiler_params=pltpu.CompilerParams(vmem_limit_bytes=vmem),
        cost_estimate=pl.CostEstimate(flops=flops, bytes_accessed=moved, transcendentals=0),
        name=name,
    )(*operands)
    return result if len(out) > 1 else result[0]


def pseudo_by_sum(input_rows, input_factor, mode_freq, mode_damping, line_freq):
    lines = line_freq.shape[0]
    columns = input_factor.shape[1] // lines
    half = columns // 2
    forced = lax.psum(
        lax.dot_general(
            input_rows, input_factor, (((0,), (0,)), ((), ())), preferred_element_type=F32
        ),
        AXES,
    )
    pieces = []
    for line in range(lines):
        gain_real, gain_imag = modal_gain(mode_freq, mode_damping, line_freq[line])
        gain_real, gain_imag = gain_real[:, None], gain_imag[:, None]
        real = forced[:, line * columns : line * columns + half]
        imag = forced[:, line * columns + half : (line + 1) * columns]
        pieces.append(gain_real * real - gain_imag * imag)
        pieces.append(gain_real * imag + gain_imag * real)
    return jnp.concatenate(pieces, axis=1).astype(BF16)


def exchange(sent, groups):
    got = lax.all_to_all(sent, AXES, 0, 0, axis_index_groups=groups)
    return got.reshape((-1,) + got.shape[2:])


def own_pseudo(input_rows, input_factor, mode_freq, mode_damping, line_freq, copies):
    devices = math.prod(FAST_SHAPE)
    rows, modes = input_rows.shape
    width = input_factor.shape[1]
    slab = modes // devices
    lines = line_freq.shape[0]
    sent, gains = call(
        pack_kernel,
        "pack",
        [((devices, 2 * rows, width), BF16), ((2 * lines, slab), F32)],
        line_freq,
        mode_freq.reshape(devices, slab),
        mode_damping.reshape(devices, slab),
        input_rows,
        input_factor,
        flops=0,
        hbm=5,
        vmem=VMEM_ALL,
        scratch=[
            pltpu.SMEM((lines,), F32),
            pltpu.VMEM((devices, slab), F32),
            pltpu.VMEM((devices, slab), F32),
            pltpu.VMEM((rows, modes), BF16),
            pltpu.VMEM((rows, width), BF16),
            pltpu.SemaphoreType.DMA((5,)),
        ],
    )
    got = lax.all_to_all(sent, AXES, 0, 0)
    return call(
        functools.partial(pseudo_kernel, rows=rows, lines=lines),
        "pseudo",
        [((copies, slab, width), BF16)],
        gains,
        got,
        flops=2 * devices * rows * slab * width,
    )


def local(
    shape,
    mode_rows,
    input_rows,
    input_factor,
    mode_freq,
    mode_damping,
    line_freq,
    boundary_rows,
    connectivity,
    stress_coef,
):
    devices = math.prod(shape)
    rows, modes = mode_rows.shape
    width = input_factor.shape[1]
    lines = line_freq.shape[0]
    exports = boundary_rows.shape[0]
    rim = exports // 2
    elems = connectivity.shape[1]
    nodes = rows + exports
    high, low = call(
        setup_kernel,
        "setup",
        [((nodes, elems), BF16)] * 2,
        connectivity,
        stress_coef,
        flops=16 * nodes * elems,
    )
    inputs = (input_rows, input_factor, mode_freq, mode_damping, line_freq)
    if shape == FAST_SHAPE and modes == devices * LANES and input_rows.shape[0] % 16 == 0:
        columns = [[z * 8 + plane for z in range(4)] for plane in range(8)]
        planes = [[z * 8 + p * 2 + c for p in range(4)] for z in range(4) for c in range(2)]
        block = exchange(own_pseudo(*inputs, copies=4), columns)
        mine = exchange(jnp.broadcast_to(block[None], (4,) + block.shape), planes)
        theirs = lax.ppermute(mine, AXES, [(i, i ^ 1) for i in range(devices)])
    else:
        pseudo = pseudo_by_sum(*inputs).reshape(2, modes // 2, width)
        core = lax.axis_index(AXES) % 2
        mine = lax.dynamic_index_in_dim(pseudo, core, 0, keepdims=False)
        theirs = lax.dynamic_index_in_dim(pseudo, 1 - core, 0, keepdims=False)
    total, others, pick = call(
        first_kernel,
        "first",
        [((rows, width), F32), ((rows, modes // 2), BF16), ((rows, exports), BF16)],
        boundary_rows.reshape(1, exports),
        mode_rows,
        mine,
        flops=rows * modes * width,
        hbm=2,
        vmem=VMEM_MOST,
        scratch=[
            pltpu.VMEM((1, exports), jnp.int32),
            pltpu.VMEM((rows, modes // 2), BF16),
            pltpu.SemaphoreType.DMA((6,)),
        ],
    )
    table, far, near = call(
        second_kernel,
        "second",
        [((width, rows), BF16), ((rim, width), BF16), ((rim, width), BF16)],
        pick,
        others,
        theirs,
        total,
        flops=rows * modes * width + 2 * exports * rows * width,
    )
    inner = [(i, i ^ 1) for i in range(devices)]
    outer = [(i, i + 1) for i in range(1, devices - 1, 2)]
    outer += [(j, i) for i, j in outer]
    near = lax.ppermute(near, AXES, inner)
    far = lax.ppermute(far, AXES, outer)
    stress = call(
        functools.partial(own_kernel, rim=rim),
        "own",
        [((width, elems), F32)],
        table,
        high,
        low,
        flops=4 * rows * elems * width,
    )
    return call(
        power_kernel,
        "power",
        [((lines, elems), F32)],
        stress,
        far,
        near,
        high,
        low,
        flops=4 * exports * elems * width,
    )


def solution(mesh):
    shape = tuple(mesh.shape[axis] for axis in AXES)
    placed = (
        P(AXES, None),
        P(AXES, None),
        P(AXES, None),
        P(),
        P(),
        P(),
        P(AXES),
        P(None, AXES),
        P(None, AXES),
    )
    return jax.shard_map(
        functools.partial(local, shape),
        mesh=mesh,
        in_specs=placed,
        out_specs=P(None, AXES),
        check_vma=False,
    )
```

time: 55.1 us -> 49.8 us (0.904)
  local copies, waits for them, and re-layouts: 6.87 us -> 1.42 us
  Pallas kernels: 4.29 us -> 7.46 us
  starting transfers between devices: 5.06 us -> 3.22 us
  waiting for transfers between devices: 3.94 us -> 2.64 us
    pallas_call x6 -> x7, Pallas kernels: 4.29 us -> 7.46 us  [call(): pl.pallas_call(kernel, out_shape=shapes, in_specs=[remains()] * hbm + [wh...]
    unnamed x12 -> x8, local copies, waits for them, and re-layouts: 4.28 us -> 1.35 us
    ppermute x2, starting transfers between devices: 5.06 us -> 3.21 us  [the longest x1 3.14 us: local(): far = lax.ppermute(far, AXES, outer)]
    reshape x3 -> x0, local copies, waits for them, and re-layouts: 1.79 us -> none  [the longest x2 1.03 us: own_pseudo(): blocks = input_rows.reshape(rows, 2, 4, 4, slab).transpose(3, 2, 1, 0, 4)]
    ppermute x2, waiting for transfers between devices: 3.93 us -> 2.64 us  [the longest x1 2.64 us: local(): far = lax.ppermute(far, AXES, outer)]
    broadcast_in_dim x3 -> x1, local copies, waits for them, and re-layouts: 0.79 us -> 0.07 us  [local(): mine = exchange(jnp.broadcast_to(block[None], (4,) + block.shape), planes)]
  transfers between devices with their start and end apart: 3 -> 3, of which waited for: 1 -> 1; matrix products, arithmetic and copies ran while one was open for 1% -> 0% of each run, Pallas kernels for 3% -> 7%
where the time goes in v3:
time: 49.8 us; the launch traced here: 49.4 us
  blocking collectives  34.6 us (69%)
  Pallas kernels  7.46 us (15%)
  starting transfers between devices  3.22 us (6%)
  waiting for transfers between devices  2.64 us (5%)
  local copies, waits for them, and re-layouts  1.42 us (3%)
    all_to_all x2, blocking collectives, exchange(): got = lax.all_to_all(sent, AXES, 0, 0, axis_index_groups=groups)  18.8 us
    all_to_all x1, blocking collectives, own_pseudo(): got = lax.all_to_all(sent, AXES, 0, 0)  15.8 us
    pallas_call x7, Pallas kernels, call(): pl.pallas_call(kernel, out_shape=shapes, in_specs=[remains()] * hbm + [wh...  7.46 us
    ppermute x1, starting transfers between devices, local(): far = lax.ppermute(far, AXES, outer)  3.14 us
    ppermute x1, waiting for transfers between devices, local(): far = lax.ppermute(far, AXES, outer)  2.64 us
    unnamed x8, local copies, waits for them, and re-layouts  1.35 us
  transfers between devices with their start and end apart: 3, of which 1 were waited for; matrix products, arithmetic and copies ran while one was open for 0% of the time, Pallas kernels for 7%

profile of v3, /device:TPU:8, one launch (start us, length us, event | category | flops | bytes accessed | tf_op | source)
XLA Modules:
  0.0 49.4 jit_solution(11952871514508601345)
XLA Ops:
  0.0 1.7 %pack.1 = (bf16[32,32,128]{2,1,0:T(8,128)(2,1)}, f32[4,128]{1,0:T(4,128)}) custom-call(f32[2]{0:T(128)} %line_hbm.1, f32[32,128]{1,0:T(8,128)} %bitcast.9, f32[32,128]{1,0:T(8,128)} %bitcast.10, bf16[16,4096]{1,0:T(8,128)(2,1)} %rows_hbm.1, bf16[16,128]{1,0:T(8,128)(2,1)} %factor_hbm.1), custom_call_target="tpu_custom_call" | custom-call | bytes 432136 | tf_op jit(solution)/shard_map/pack/pallas_call | solution.py:200
  1.7 15.8 %all_to_all.15.got_ref = bf16[32,32,128]{2,1,0:T(8,128)(2,1)S(1)} all-to-all(bf16[32,32,128]{2,1,0:T(8,128)(2,1)} %get-tuple-element.16), channel_id=1, replica_groups=mesh['region'=8,'sub'=4] {'region','sub'}, dimensions={0} | all-to-all | bytes 524288 | tf_op jit(solution)/shard_map/all_to_all | solution.py:266
  17.5 0.0 copy-start
  17.5 0.7 %copy-done = f32[4,128]{1,0:T(4,128)S(1)} copy-done((f32[4,128]{1,0:T(4,128)S(1)}, f32[4,128]{1,0:T(4,128)}, u32[]{:S(2)}) %copy-start) | copy-done | bytes 2072
  18.2 0.3 pseudo.1
  18.5 8.7 %all_to_all.16 = bf16[4,128,128]{2,1,0:T(8,128)(2,1)S(1)} all-to-all(bf16[4,128,128]{2,1,0:T(8,128)(2,1)S(1)} %pseudo.1), channel_id=1, replica_groups={{0,8,16,24},{1,9,17,25},{2,10,18,26},{3,11,19,27},{4,12,20,28},{5,13,21..., dimensions={0} | all-to-all | bytes 262144 | tf_op jit(solution)/shard_map/all_to_all | solution.py:235
  27.2 0.1 broadcast_in_dim.8
  27.3 0.0 copy-start.2
  27.3 0.0 copy-start.3
  27.3 10.1 %all_to_all.17 = bf16[4,512,128]{2,1,0:T(8,128)(2,1)S(1)} all-to-all(bf16[4,512,128]{2,1,0:T(8,128)(2,1)S(1)} %broadcast_in_dim.8), channel_id=1, replica_groups={{0,2,4,6},{1,3,5,7},{8,10,12,14},{9,11,13,15},{16,18,20,22},{17,19,21,2..., dimensions={0} | all-to-all | bytes 1048576 | tf_op jit(solution)/shard_map/all_to_all | solution.py:235
  37.4 0.0 collective-permute-start
  37.4 0.0 copy-start.1
  37.4 0.7 %copy-done.1 = s32[128]{0:T(128)S(1)} copy-done((s32[128]{0:T(128)S(1)}, s32[128]{0:T(128)}, u32[]{:S(2)}) %copy-start.1) | copy-done | bytes 536
  38.1 2.7 %first.1 = (f32[512,128]{1,0:T(8,128)S(1)}, bf16[512,2048]{1,0:T(8,128)(2,1)S(1)}, bf16[512,128]{1,0:T(8,128)(2,1)S(1)}) custom-call(s32[1,128]{1,0:T(1,128)S(1)} %bitcast.7, bf16[512,4096]{1,0:T(8,128)(2,1)} %modes_hbm.1, bf16[2048,128]{1,0:T(8,128)(2,1)S(1)} %bitcast.6), custom_call_target="tpu_custom_call" | custom-call | flops 268435456 | bytes 7209472 | tf_op jit(solution)/shard_map/first/pallas_call | solution.py:200
  40.8 0.0 collective-permute-done.pseudo_ref
  40.8 0.9 %second.1 = (bf16[128,512]{1,0:T(8,128)(2,1)S(1)}, bf16[64,128]{1,0:T(8,128)(2,1)S(1)}, bf16[64,128]{1,0:T(8,128)(2,1)S(1)}) custom-call(bf16[512,128]{1,0:T(8,128)(2,1)S(1)} %get-tuple-element.17.pick_ref, bf16[512,2048]{1,0:T(8,128)(2,1)S(1)} %get-tuple-element.18.modes_ref, bf16[2048,128]{1,0:T(8,128)(2,1)S(1)} %collective-permute-done.pseudo_ref, ...), custom_call_target="tpu_custom_call" | custom-call | flops 285212672 | bytes 3178496 | tf_op jit(solution)/shard_map/second/pallas_call | solution.py:200
  41.7 3.1 %collective-permute-start.1 = (bf16[64,128]{1,0:T(8,128)(2,1)S(1)}, bf16[64,128]{1,0:T(8,128)(2,1)S(1)}, u32[]{:S(2)}, u32[]{:S(2)}) collective-permute-start(bf16[64,128]{1,0:T(8,128)(2,1)S(1)} %get-tuple-element.23), channel_id=1, source_target_pairs={{1,2},{3,4},{5,6},{7,8},{9,10},{11,12},{13,14},{15,16},{17,18},{19... | collective-permute-start | bytes 49160 | tf_op jit(solution)/shard_map/ppermute | solution.py:347
  44.8 0.1 collective-permute-start.2
  44.9 0.0 copy-done.2
  44.9 0.0 copy-done.3
  44.9 0.7 %setup.1 = (bf16[640,512]{1,0:T(8,128)(2,1)S(1)}, bf16[640,512]{1,0:T(8,128)(2,1)S(1)}) custom-call(s32[4,512]{1,0:T(4,128)S(1)} %copy-done.2, f32[4,512]{1,0:T(4,128)S(1)} %copy-done.3), custom_call_target="tpu_custom_call" | custom-call | flops 5242880 | bytes 1327104 | tf_op jit(solution)/shard_map/setup/pallas_call | solution.py:200
  45.6 0.3 own.1.stress_ref
  45.9 2.6 %collective-permute-done.1.far_ref = bf16[64,128]{1,0:T(8,128)(2,1)S(1)} collective-permute-done((bf16[64,128]{1,0:T(8,128)(2,1)S(1)}, bf16[64,128]{1,0:T(8,128)(2,1)S(1)}, u32[]{:S(2)}, u32[]{:S(2)}) %collective-permute-start.1) | collective-permute-done | bytes 16416 | tf_op jit(solution)/shard_map/ppermute | solution.py:347
  48.5 0.0 collective-permute-done.2.near_ref
  48.5 0.9 %power.1 = f32[2,512]{1,0:T(2,128)} custom-call(f32[128,512]{1,0:T(8,128)S(1)} %own.1.stress_ref, bf16[64,128]{1,0:T(8,128)(2,1)S(1)} %collective-permute-done.1.far_ref, bf16[64,128]{1,0:T(8,128)(2,1)S(1)} %collective-permute-done.2.near_ref, bf16[640,512]{1,0:T(8,128)(2,1)S(1)} %get-tuple-element.21.high_ref, bf16[640,512]{1,0:T(8,128)(2,1)S(1)} %get-tuple-element.22.low_ref), custom_call_target="tpu_custom_call" | custom-call | flops 33554432 | bytes 1609728 | tf_op jit(solution)/shard_map/power/pallas_call | solution.py:200
Async XLA Ops:
  17.5 0.7 %copy-start = (f32[4,128]{1,0:T(4,128)S(1)}, f32[4,128]{1,0:T(4,128)}, u32[]{:S(2)}) copy-start(f32[4,128]{1,0:T(4,128)} %get-tuple-element.15.gain_ref) | copy-start | bytes 6148
  27.3 17.6 %copy-start.2 = (s32[4,512]{1,0:T(4,128)S(1)}, s32[4,512]{1,0:T(4,128)}, u32[]{:S(2)}) copy-start(s32[4,512]{1,0:T(4,128)} %connect_ref.1) | copy-start | bytes 24580
  27.3 17.6 %copy-start.3 = (f32[4,512]{1,0:T(4,128)S(1)}, f32[4,512]{1,0:T(4,128)}, u32[]{:S(2)}) copy-start(f32[4,512]{1,0:T(4,128)} %coef_ref.1) | copy-start | bytes 24580
  37.4 3.4 %collective-permute-start = (bf16[2048,128]{1,0:T(8,128)(2,1)S(1)}, bf16[2048,128]{1,0:T(8,128)(2,1)S(1)}, u32[]{:S(2)}, u32[]{:S(2)}) collective-permute-start(bf16[2048,128]{1,0:T(8,128)(2,1)S(1)} %bitcast.5), channel_id=1, source_target_pairs={{0,1},{1,0},{2,3},{3,2},{4,5},{5,4},{6,7},{7,6},{8,9},{9,8},{10,11... | collective-permute-start | bytes 1572872 | tf_op jit(solution)/shard_map/ppermute | solution.py:311
  37.4 0.7 %copy-start.1 = (s32[128]{0:T(128)S(1)}, s32[128]{0:T(128)}, u32[]{:S(2)}) copy-start(s32[128]{0:T(128)} %param.15) | copy-start | bytes 1540
  41.7 6.9 %collective-permute-start.1 = (bf16[64,128]{1,0:T(8,128)(2,1)S(1)}, bf16[64,128]{1,0:T(8,128)(2,1)S(1)}, u32[]{:S(2)}, u32[]{:S(2)}) collective-permute-start(bf16[64,128]{1,0:T(8,128)(2,1)S(1)} %get-tuple-element.23), channel_id=1, source_target_pairs={{1,2},{3,4},{5,6},{7,8},{9,10},{11,12},{13,14},{15,16},{17,18},{19... | collective-permute-start | bytes 49160 | tf_op jit(solution)/shard_map/ppermute | solution.py:347
  44.8 3.7 %collective-permute-start.2 = (bf16[64,128]{1,0:T(8,128)(2,1)S(1)}, bf16[64,128]{1,0:T(8,128)(2,1)S(1)}, u32[]{:S(2)}, u32[]{:S(2)}) collective-permute-start(bf16[64,128]{1,0:T(8,128)(2,1)S(1)} %get-tuple-element.24), channel_id=1, source_target_pairs={{0,1},{1,0},{2,3},{3,2},{4,5},{5,4},{6,7},{7,6},{8,9},{9,8},{10,11... | collective-permute-start | bytes 49160 | tf_op jit(solution)/shard_map/ppermute | solution.py:346
